TPU v7x, 32 devices: a whole 2x2x4 slice. The times are simulated.
32 devices in a mesh: seq: 8 (over z, core), mp: 4 (over y, x).
Axes of the slice: x: 2, y: 2, z: 4, core: 2. Of those that a mesh axis runs over, the one named last changes fastest.
Arguments:
- tokens: bfloat16 [128, 8192], P('seq', 'mp'), may hold values from -6 to 6
- gate_code: bfloat16 [8192, 16384], P('mp', 'seq'), may hold values from -4 to 4
- gate_scale: float32 [64, 128], P('mp', 'seq'), may hold values from 0.0055242716 to 0.022097087
- up_code: bfloat16 [8192, 16384], P('mp', 'seq'), may hold values from -4 to 4
- up_scale: float32 [64, 128], P('mp', 'seq'), may hold values from 0.0055242716 to 0.022097087
- down_code: bfloat16 [16384, 8192], P('seq', 'mp'), may hold values from -4 to 4
- down_scale: float32 [128, 64], P('seq', 'mp'), may hold values from 0.0078125 to 0.03125
Outputs:
- mixed: bfloat16 [128, 8192], P('seq', 'mp')
All inputs are finite; a program needn't handle non-finite values.
Results may differ from a plain program's by a relative error of at most 0.0071.
Values may be sent and summed in bfloat16 or wider, within the bound.
A program may use at most 128 MiB of HBM per device.

v0:
```python
import functools

import jax
import jax.numpy as jnp
from jax import lax
from jax.experimental import pallas as pl
from jax.experimental.pallas import tpu as pltpu
from jax.sharding import PartitionSpec as P

MESH = pl.DeviceIdType.MESH
BF16 = jnp.bfloat16
F32 = jnp.float32


def chunk_of(units):
    return 512 if units % 512 == 0 else units


def kernel(n, m, tok_hbm, wg_hbm, wu_hbm, wd_hbm, gs, us, ds, out,
           tok, wg, wu, wd, part, rsr, hid, acc, dsend, sibr, zs, zr,
           w_sem, t_loc, t_send, t_recv, f_send, f_recv,
           r_send, r_recv, h_send, h_recv, b_send, b_recv, z_send, z_recv):
    seq, mp = lax.axis_index("seq"), lax.axis_index("mp")
    nz = n // 2
    z, core = seq // 2, lax.rem(seq, 2)
    sib = z * 2 + (1 - core)
    rows_in, feats = tok_hbm.shape
    units = wg.shape[1]
    w = chunk_of(units)
    chunks = units // w
    tokens = n * rows_in
    outs = wd.shape[1]
    v = chunk_of(outs)
    vparts = outs // v
    block = feats // gs.shape[0]

    loads = {}
    for c in range(chunks):
        cols = pl.ds(c * w, w)
        for k, (src, dst) in enumerate(((wg_hbm, wg), (wu_hbm, wu))):
            loads[k, c] = pltpu.make_async_copy(src.at[:, cols], dst.at[:, cols], w_sem.at[k, c])
            loads[k, c].start()
    for c in range(chunks):
        rows = pl.ds(c * w, w)
        loads[2, c] = pltpu.make_async_copy(wd_hbm.at[rows], wd.at[rows], w_sem.at[2, c])
        loads[2, c].start()

    barrier = pltpu.get_barrier_semaphore()

    def z_peer(d):
        return lax.rem(z + d, nz) * 2 + core

    def mp_peer(d):
        return lax.rem(mp + d, m)

    for d in range(1, nz):
        pl.semaphore_signal(barrier, inc=1, device_id=(z_peer(d), mp), device_id_type=MESH)
    pl.semaphore_signal(barrier, inc=1, device_id=(sib, mp), device_id_type=MESH)
    for d in range(1, m):
        pl.semaphore_signal(barrier, inc=1, device_id=(seq, mp_peer(d)), device_id_type=MESH)
    pl.semaphore_wait(barrier, nz + m - 1)

    def remote(src, dst, ssem, rsem, to):
        return pltpu.make_async_remote_copy(
            src_ref=src, dst_ref=dst, send_sem=ssem, recv_sem=rsem,
            device_id=to, device_id_type=MESH)

    sends = []

    def tok_rows(s):
        return tok.at[pl.ds(pl.multiple_of(s * rows_in, rows_in), rows_in)]

    own = pltpu.make_async_copy(tok_hbm, tok_rows(seq), t_loc)
    own.start()
    t_copies = []
    for d in range(1, nz):
        cp = remote(tok_hbm, tok_rows(seq), t_send.at[d - 1], t_recv.at[d - 1], (z_peer(d), mp))
        cp.start()
        t_copies.append(cp)
        sends.append(cp)
    f_copies = []
    cp = remote(tok_hbm, tok_rows(seq), f_send.at[0], f_recv.at[0], (sib, mp))
    cp.start()
    f_copies.append(cp)
    sends.append(cp)

    def dequant(ref, scale, row0, nrows, col0, ncols):
        def body(i, carry):
            kb = row0 // block + i
            rows = pl.ds(pl.multiple_of(kb * block, block), block)
            for nb in range(col0 // block, (col0 + ncols) // block):
                cols = pl.ds(nb * block, block)
                ref[rows, cols] = (ref[rows, cols].astype(F32) * scale[kb, nb]).astype(BF16)
            return carry
        lax.fori_loop(0, nrows // block, body, 0)

    def prepare(c):
        loads[0, c].wait()
        dequant(wg, gs, 0, feats, c * w, w)
        loads[1, c].wait()
        dequant(wu, us, 0, feats, c * w, w)

    prepare(0)

    own.wait()
    for d in range(1, nz):
        t_copies[d - 1].wait_recv()
        s = lax.rem(z - d + nz, nz) * 2 + core
        cp = remote(tok_rows(s), tok_rows(s), f_send.at[d], f_recv.at[d], (sib, mp))
        cp.start()
        f_copies.append(cp)
        sends.append(cp)
    for cp in f_copies:
        cp.wait_recv()

    rows_mp = tokens // m

    def first(c):
        x = tok[...]
        g = jnp.dot(x, wg[:, c * w:(c + 1) * w], preferred_element_type=F32)
        part[c, :, :, :w] = g.astype(BF16).reshape(m, rows_mp, w)
        u = jnp.dot(x, wu[:, c * w:(c + 1) * w], preferred_element_type=F32)
        part[c, :, :, w:] = u.astype(BF16).reshape(m, rows_mp, w)
        copies = []
        for d in range(1, m):
            to = mp_peer(d)
            cp = remote(part.at[c, to], rsr.at[c, d - 1], r_send.at[c, d - 1],
                        r_recv.at[c, d - 1], (seq, to))
            cp.start()
            copies.append(cp)
            sends.append(cp)
        return copies

    def middle(c, copies):
        total = part[c, mp].astype(F32)
        for d in range(1, m):
            copies[d - 1].wait_recv()
            total += rsr[c, d - 1].astype(F32)
        g, u = total[:, :w], total[:, w:]
        hid[c, mp] = (g / (1.0 + jnp.exp(-g)) * u).astype(BF16)
        out_copies = []
        for d in range(1, m):
            to = mp_peer(d)
            cp = remote(hid.at[c, mp], hid.at[c, mp], h_send.at[c, d - 1],
                        h_recv.at[c, d - 1], (seq, to))
            cp.start()
            out_copies.append(cp)
            sends.append(cp)
        return out_copies

    def down(c, j):
        h = hid[c].reshape(tokens, w)
        y = jnp.dot(h, wd[c * w:(c + 1) * w, j * v:(j + 1) * v], preferred_element_type=F32)
        y = y.reshape(nz, 2, rows_in, v)
        acc[j] = y if c == 0 else acc[j] + y

    def down_all(c, copies):
        for cp in copies:
            cp.wait_recv()
        for j in range(vparts):
            down(c, j)

    rs, ag = {}, {}
    for c in range(chunks):
        if c > 0:
            prepare(c)
        rs[c] = first(c)
        loads[2, c].wait()
        dequant(wd, ds, c * w, w, 0, outs)
        if c >= 1:
            ag[c - 1] = middle(c - 1, rs[c - 1])
        if c >= 2:
            down_all(c - 2, ag[c - 2])
    last = chunks - 1
    ag[last] = middle(last, rs[last])
    if last >= 1:
        down_all(last - 1, ag[last - 1])

    for cp in ag[last]:
        cp.wait_recv()
    b_copies, z_copies = [], {}

    def across(j):
        b_copies[j].wait_recv()
        zs[j] = (acc[j, :, core] + sibr[j].astype(F32)).astype(BF16)
        for d in range(1, nz):
            cp = remote(zs.at[j, lax.rem(z + d, nz)], zr.at[j, d - 1], z_send.at[j, d - 1],
                        z_recv.at[j, d - 1], (z_peer(d), mp))
            cp.start()
            z_copies[j, d] = cp
            sends.append(cp)

    for j in range(vparts):
        down(last, j)
        dsend[j] = acc[j, :, 1 - core].astype(BF16)
        cp = remote(dsend.at[j], sibr.at[j], b_send.at[j], b_recv.at[j], (sib, mp))
        cp.start()
        b_copies.append(cp)
        sends.append(cp)
        if j >= 1:
            across(j - 1)
    across(vparts - 1)

    for j in range(vparts):
        total = acc[j, z, core] + sibr[j, z].astype(F32)
        for d in range(1, nz):
            z_copies[j, d].wait_recv()
            total += zr[j, d - 1].astype(F32)
        out[:, j * v:(j + 1) * v] = total.astype(BF16)

    for cp in sends:
        cp.wait_send()


def shards(n, m, tokens, gate_code, gate_scale, up_code, up_scale, down_code, down_scale):
    rows_in, feats = tokens.shape
    units, outs = gate_code.shape[1], down_code.shape[1]
    total = n * rows_in
    w, v = chunk_of(units), chunk_of(outs)
    chunks, vparts = units // w, outs // v
    nz, rows_mp = n // 2, total // m
    dma = pltpu.SemaphoreType.DMA
    hbm = pl.BlockSpec(memory_space=pl.ANY)
    smem = pl.BlockSpec(memory_space=pltpu.SMEM)
    return pl.pallas_call(
        functools.partial(kernel, n, m),
        out_shape=jax.ShapeDtypeStruct((rows_in, outs), BF16),
        in_specs=[hbm] * 4 + [smem] * 3,
        out_specs=pl.BlockSpec(memory_space=pltpu.VMEM),
        scratch_shapes=[
            pltpu.VMEM((total, feats), BF16),
            pltpu.VMEM((feats, units), BF16),
            pltpu.VMEM((feats, units), BF16),
            pltpu.VMEM((units, outs), BF16),
            pltpu.VMEM((chunks, m, rows_mp, 2 * w), BF16),
            pltpu.VMEM((chunks, m - 1, rows_mp, 2 * w), BF16),
            pltpu.VMEM((chunks, m, rows_mp, w), BF16),
            pltpu.VMEM((vparts, nz, 2, rows_in, v), F32),
            pltpu.VMEM((vparts, nz, rows_in, v), BF16),
            pltpu.VMEM((vparts, nz, rows_in, v), BF16),
            pltpu.VMEM((vparts, nz, rows_in, v), BF16),
            pltpu.VMEM((vparts, nz - 1, rows_in, v), BF16),
            dma((3, chunks)),
            dma,
            dma((nz - 1,)), dma((nz - 1,)),
            dma((nz,)), dma((nz,)),
            dma((chunks, m - 1)), dma((chunks, m - 1)),
            dma((chunks, m - 1)), dma((chunks, m - 1)),
            dma((vparts,)), dma((vparts,)),
            dma((vparts, nz - 1)), dma((vparts, nz - 1)),
        ],
        compiler_params=pltpu.CompilerParams(
            collective_id=0, has_side_effects=True, vmem_limit_bytes=58 * 1024 * 1024),
    )(tokens, gate_code, up_code, down_code, gate_scale, up_scale, down_scale)


def solution(mesh):
    placed = (
        P("seq", "mp"),
        P("mp", "seq"),
        P("mp", "seq"),
        P("mp", "seq"),
        P("mp", "seq"),
        P("seq", "mp"),
        P("seq", "mp"),
    )
    body = functools.partial(shards, mesh.shape["seq"], mesh.shape["mp"])
    return jax.shard_map(
        body, mesh=mesh, in_specs=placed, out_specs=P("seq", "mp"), check_vma=False
    )
```

profile of v0, /device:TPU:1, one launch (start us, length us, event | category | flops | bytes accessed | tf_op | source)
XLA Modules:
  0.0 46.9 jit_solution(11152621247019159816)
XLA Ops:
  0.0 45.4 %shard_map.73 = bf16[16,2048]{1,0:T(8,128)(2,1)} custom-call(bf16[16,2048]{1,0:T(8,128)(2,1)} %tok_hbm.1, bf16[2048,2048]{1,0:T(8,128)(2,1)} %wg_hbm.1, bf16[2048,2048]{1,0:T(8,128)(2,1)} %wu_hbm.1, bf16[2048,2048]{1,0:T(8,128)(2,1)} %wd_hbm.1, f32[16,16]{1,0:T(8,128)} %gs.1, f32[16,16]{1,0:T(8,128)} %us.1, f32[16,16]{1,0:T(8,128)} %ds.1), custom_call_target="tpu_custom_call" | custom-call | tf_op jit(solution)/shard_map/pallas_call | solution.py:225
  45.4 1.5 %copy.9 = bf16[16,2048]{1,0:T(8,128)(2,1)} copy(bf16[16,2048]{1,0:T(8,128)(2,1)} %shard_map.73) | data formatting | bytes 131072
where the time goes:
time: 47.4 us; the launch traced here: 46.9 us
  Pallas kernels  45.4 us (96%)
  local copies, waits for them, and re-layouts  1.47 us (3%)
    pallas_call x1, Pallas kernels, shards(): pl.pallas_call(functools.partial(kernel, n, m), out_shape=jax.ShapeDtypeS...  45.4 us
    unnamed x1, local copies, waits for them, and re-layouts  1.47 us

commit v1 on v0

v1 whole, which is shorter than its diff:
```python
import functools

import jax
import jax.numpy as jnp
from jax import lax
from jax.experimental import pallas as pl
from jax.experimental.pallas import tpu as pltpu
from jax.sharding import PartitionSpec as P

MESH = pl.DeviceIdType.MESH
BF16 = jnp.bfloat16
F32 = jnp.float32


def chunk_of(units):
    return 512 if units % 512 == 0 else units


def units_of(units):
    return 1024 if units % 1024 == 0 else units


def kernel(n, m, tok_hbm, wg_hbm, wu_hbm, wd_hbm, gs, us, ds, out,
           tok, wg, wu, wd, part, rsr, hid, acc, dsend, sibr, zs, zr,
           w_sem, t_loc, t_send, t_recv, f_send, f_recv,
           r_send, r_recv, h_send, h_recv, b_send, b_recv, z_send, z_recv):
    seq, mp = lax.axis_index("seq"), lax.axis_index("mp")
    nz = n // 2
    z, core = seq // 2, lax.rem(seq, 2)
    sib = z * 2 + (1 - core)
    rows_in, feats = tok_hbm.shape
    units = wg.shape[1]
    w = units_of(units)
    chunks = units // w
    tokens = n * rows_in
    outs = wd.shape[1]
    v = chunk_of(outs)
    vparts = outs // v
    block = feats // gs.shape[0]

    loads = {}

    def load(k, c):
        span = pl.ds(c * w, w)
        src, dst = ((wg_hbm, wg), (wu_hbm, wu), (wd_hbm, wd))[k]
        src, dst = (src.at[span], dst.at[span]) if k == 2 else (src.at[:, span], dst.at[:, span])
        loads[k, c] = pltpu.make_async_copy(src, dst, w_sem.at[k, c])
        loads[k, c].start()

    load(0, 0)
    load(1, 0)

    barrier = pltpu.get_barrier_semaphore()

    def z_peer(d):
        return lax.rem(z + d, nz) * 2 + core

    def mp_peer(d):
        return lax.rem(mp + d, m)

    for d in range(1, nz):
        pl.semaphore_signal(barrier, inc=1, device_id=(z_peer(d), mp), device_id_type=MESH)
    pl.semaphore_signal(barrier, inc=1, device_id=(sib, mp), device_id_type=MESH)
    for d in range(1, m):
        pl.semaphore_signal(barrier, inc=1, device_id=(seq, mp_peer(d)), device_id_type=MESH)
    pl.semaphore_wait(barrier, nz + m - 1)

    def remote(src, dst, ssem, rsem, to):
        return pltpu.make_async_remote_copy(
            src_ref=src, dst_ref=dst, send_sem=ssem, recv_sem=rsem,
            device_id=to, device_id_type=MESH)

    sends = []

    def tok_rows(s):
        return tok.at[lax.rem(s, 2), pl.ds(pl.multiple_of(s // 2 * rows_in, rows_in), rows_in)]

    own = pltpu.make_async_copy(tok_hbm, tok_rows(seq), t_loc)
    own.start()
    t_copies = []
    for d in range(1, nz):
        cp = remote(tok_hbm, tok_rows(seq), t_send.at[d - 1], t_recv.at[d - 1], (z_peer(d), mp))
        cp.start()
        t_copies.append(cp)
        sends.append(cp)
    f_copies = []
    cp = remote(tok_hbm, tok_rows(seq), f_send.at[0], f_recv.at[0], (sib, mp))
    cp.start()
    f_copies.append(cp)
    sends.append(cp)

    for c in range(1, chunks):
        load(0, c)
        load(1, c)
    for c in range(chunks):
        load(2, c)

    def dequant(ref, scale, row0, nrows, col0, ncols):
        def body(i, carry):
            kb = row0 // block + i
            rows = pl.ds(pl.multiple_of(kb * block, block), block)
            for nb in range(col0 // block, (col0 + ncols) // block):
                cols = pl.ds(nb * block, block)
                ref[rows, cols] = (ref[rows, cols].astype(F32) * scale[kb, nb]).astype(BF16)
            return carry
        lax.fori_loop(0, nrows // block, body, 0)

    def prepare(c):
        loads[0, c].wait()
        dequant(wg, gs, 0, feats, c * w, w)
        loads[1, c].wait()
        dequant(wu, us, 0, feats, c * w, w)

    prepare(0)

    own.wait()
    for d in range(1, nz):
        t_copies[d - 1].wait_recv()
        s = lax.rem(z - d + nz, nz) * 2 + core
        cp = remote(tok_rows(s), tok_rows(s), f_send.at[d], f_recv.at[d], (sib, mp))
        cp.start()
        f_copies.append(cp)
        sends.append(cp)
    for cp in f_copies:
        cp.wait_recv()

    half = tokens // 2
    rows_mp = half // m

    def first(h, c):
        x = tok[h]
        g = jnp.dot(x, wg[:, c * w:(c + 1) * w], preferred_element_type=F32)
        part[h, c, :, :, :w] = g.astype(BF16).reshape(m, rows_mp, w)
        u = jnp.dot(x, wu[:, c * w:(c + 1) * w], preferred_element_type=F32)
        part[h, c, :, :, w:] = u.astype(BF16).reshape(m, rows_mp, w)
        copies = []
        for d in range(1, m):
            to = mp_peer(d)
            cp = remote(part.at[h, c, to], rsr.at[h, c, d - 1], r_send.at[h, c, d - 1],
                        r_recv.at[h, c, d - 1], (seq, to))
            cp.start()
            copies.append(cp)
            sends.append(cp)
        rs[h, c] = copies

    def middle(h, c):
        total = part[h, c, mp].astype(F32)
        for d in range(1, m):
            rs[h, c][d - 1].wait_recv()
            total += rsr[h, c, d - 1].astype(F32)
        g, u = total[:, :w], total[:, w:]
        hid[h, c, mp] = (g / (1.0 + jnp.exp(-g)) * u).astype(BF16)
        copies = []
        for d in range(1, m):
            to = mp_peer(d)
            cp = remote(hid.at[h, c, mp], hid.at[h, c, mp], h_send.at[h, c, d - 1],
                        h_recv.at[h, c, d - 1], (seq, to))
            cp.start()
            copies.append(cp)
            sends.append(cp)
        ag[h, c] = copies

    def down(h, c, j):
        x = hid[h, c].reshape(half, w)
        y = jnp.dot(x, wd[c * w:(c + 1) * w, j * v:(j + 1) * v], preferred_element_type=F32)
        y = y.reshape(nz, rows_in, v)
        acc[h, j] = y if c == 0 else acc[h, j] + y

    def to_sibling(j):
        return remote(dsend.at[j], sibr.at[j], b_send.at[j], b_recv.at[j], (sib, mp))

    def to_z(j, d):
        return remote(zs.at[j, lax.rem(z + d, nz)], zr.at[j, d - 1], z_send.at[j, d - 1],
                      z_recv.at[j, d - 1], (z_peer(d), mp))

    def down_half(h):
        for c in range(chunks - 1):
            for cp in ag[h, c]:
                cp.wait_recv()
            for j in range(vparts):
                down(h, c, j)
        for cp in ag[h, chunks - 1]:
            cp.wait_recv()
        for j in range(vparts):
            down(h, chunks - 1, j)

            @pl.when(core == 1 - h)
            def _():
                dsend[j] = acc[h, j].astype(BF16)
                to_sibling(j).start()

    def across(h):
        @pl.when(core == h)
        def _():
            for j in range(vparts):
                to_sibling(j).wait_recv()
                zs[j] = (acc[h, j] + sibr[j].astype(F32)).astype(BF16)
                for d in range(1, nz):
                    to_z(j, d).start()

    rs, ag = {}, {}
    for c in range(chunks):
        if c > 0:
            prepare(c)
        first(0, c)
    for c in range(chunks):
        first(1, c)
        middle(0, c)
    for c in range(chunks):
        loads[2, c].wait()
        dequant(wd, ds, c * w, w, 0, outs)
    for c in range(chunks):
        middle(1, c)
    down_half(0)
    across(0)
    down_half(1)
    across(1)

    for j in range(vparts):
        total = acc[core, j, z] + sibr[j, z].astype(F32)
        for d in range(1, nz):
            to_z(j, d).wait_recv()
            total += zr[j, d - 1].astype(F32)
        out[:, j * v:(j + 1) * v] = total.astype(BF16)

    for j in range(vparts):
        to_sibling(j).wait_send()
        for d in range(1, nz):
            to_z(j, d).wait_send()
    for cp in sends:
        cp.wait_send()


def shards(n, m, tokens, gate_code, gate_scale, up_code, up_scale, down_code, down_scale):
    rows_in, feats = tokens.shape
    units, outs = gate_code.shape[1], down_code.shape[1]
    total = n * rows_in
    w, v = units_of(units), chunk_of(outs)
    chunks, vparts = units // w, outs // v
    nz, rows_mp = n // 2, total // 2 // m
    dma = pltpu.SemaphoreType.DMA
    hbm = pl.BlockSpec(memory_space=pl.ANY)
    smem = pl.BlockSpec(memory_space=pltpu.SMEM)
    return pl.pallas_call(
        functools.partial(kernel, n, m),
        out_shape=jax.ShapeDtypeStruct((rows_in, outs), BF16),
        in_specs=[hbm] * 4 + [smem] * 3,
        out_specs=pl.BlockSpec(memory_space=pltpu.VMEM),
        scratch_shapes=[
            pltpu.VMEM((2, total // 2, feats), BF16),
            pltpu.VMEM((feats, units), BF16),
            pltpu.VMEM((feats, units), BF16),
            pltpu.VMEM((units, outs), BF16),
            pltpu.VMEM((2, chunks, m, rows_mp, 2 * w), BF16),
            pltpu.VMEM((2, chunks, m - 1, rows_mp, 2 * w), BF16),
            pltpu.VMEM((2, chunks, m, rows_mp, w), BF16),
            pltpu.VMEM((2, vparts, nz, rows_in, v), F32),
            pltpu.VMEM((vparts, nz, rows_in, v), BF16),
            pltpu.VMEM((vparts, nz, rows_in, v), BF16),
            pltpu.VMEM((vparts, nz, rows_in, v), BF16),
            pltpu.VMEM((vparts, nz - 1, rows_in, v), BF16),
            dma((3, chunks)),
            dma,
            dma((nz - 1,)), dma((nz - 1,)),
            dma((nz,)), dma((nz,)),
            dma((2, chunks, m - 1)), dma((2, chunks, m - 1)),
            dma((2, chunks, m - 1)), dma((2, chunks, m - 1)),
            dma((vparts,)), dma((vparts,)),
            dma((vparts, nz - 1)), dma((vparts, nz - 1)),
        ],
        compiler_params=pltpu.CompilerParams(
            collective_id=0, has_side_effects=True, vmem_limit_bytes=58 * 1024 * 1024),
    )(tokens, gate_code, up_code, down_code, gate_scale, up_scale, down_scale)


def solution(mesh):
    placed = (
        P("seq", "mp"),
        P("mp", "seq"),
        P("mp", "seq"),
        P("mp", "seq"),
        P("mp", "seq"),
        P("seq", "mp"),
        P("seq", "mp"),
    )
    body = functools.partial(shards, mesh.shape["seq"], mesh.shape["mp"])
    return jax.shard_map(
        body, mesh=mesh, in_specs=placed, out_specs=P("seq", "mp"), check_vma=False
    )
```

time: 47.4 us -> 45.6 us (0.962)
  Pallas kernels: 45.4 us -> 43.9 us
    pallas_call x1, Pallas kernels: 45.4 us -> 43.9 us  [shards(): pl.pallas_call(functools.partial(kernel, n, m), out_shape=jax.ShapeDtypeS...]
where the time goes in v1:
time: 45.6 us; the launch traced here: 45.4 us
  Pallas kernels  43.9 us (96%)
  local copies, waits for them, and re-layouts  1.47 us (3%)
    pallas_call x1, Pallas kernels, shards(): pl.pallas_call(functools.partial(kernel, n, m), out_shape=jax.ShapeDtypeS...  43.9 us
    unnamed x1, local copies, waits for them, and re-layouts  1.47 us

profile of v1, /device:TPU:1, one launch (start us, length us, event | category | flops | bytes accessed | tf_op | source)
XLA Modules:
  0.0 45.4 jit_solution(11622877811238196833)
XLA Ops:
  0.0 43.9 %shard_map.73 = bf16[16,2048]{1,0:T(8,128)(2,1)} custom-call(bf16[16,2048]{1,0:T(8,128)(2,1)} %tok_hbm.1, bf16[2048,2048]{1,0:T(8,128)(2,1)} %wg_hbm.1, bf16[2048,2048]{1,0:T(8,128)(2,1)} %wu_hbm.1, bf16[2048,2048]{1,0:T(8,128)(2,1)} %wd_hbm.1, f32[16,16]{1,0:T(8,128)} %gs.1, f32[16,16]{1,0:T(8,128)} %us.1, f32[16,16]{1,0:T(8,128)} %ds.1), custom_call_target="tpu_custom_call" | custom-call | tf_op jit(solution)/shard_map/pallas_call | solution.py:244
  43.9 1.5 %copy.9 = bf16[16,2048]{1,0:T(8,128)(2,1)} copy(bf16[16,2048]{1,0:T(8,128)(2,1)} %shard_map.73) | data formatting | bytes 131072

commit v2 on v1

--- a/solution.py
+++ b/solution.py
@@ -203,12 +203,11 @@
         if c > 0:
             prepare(c)
         first(0, c)
-    for c in range(chunks):
         first(1, c)
-        middle(0, c)
     for c in range(chunks):
         loads[2, c].wait()
         dequant(wd, ds, c * w, w, 0, outs)
+        middle(0, c)
     for c in range(chunks):
         middle(1, c)
     down_half(0)

time: 45.6 us -> 44.3 us (0.971)
  Pallas kernels: 43.9 us -> 42.7 us
    pallas_call x1, Pallas kernels: 43.9 us -> 42.7 us  [shards(): pl.pallas_call(functools.partial(kernel, n, m), out_shape=jax.ShapeDtypeS...]
where the time goes in v2:
time: 44.3 us; the launch traced here: 44.1 us
  Pallas kernels  42.7 us (96%)
  local copies, waits for them, and re-layouts  1.47 us (3%)
    pallas_call x1, Pallas kernels, shards(): pl.pallas_call(functools.partial(kernel, n, m), out_shape=jax.ShapeDtypeS...  42.7 us
    unnamed x1, local copies, waits for them, and re-layouts  1.47 us

profile of v2, /device:TPU:1, one launch (start us, length us, event | category | flops | bytes accessed | tf_op | source)
XLA Modules:
  0.0 44.1 jit_solution(18036926646913079942)
XLA Ops:
  0.0 42.7 %shard_map.73 = bf16[16,2048]{1,0:T(8,128)(2,1)} custom-call(bf16[16,2048]{1,0:T(8,128)(2,1)} %tok_hbm.1, bf16[2048,2048]{1,0:T(8,128)(2,1)} %wg_hbm.1, bf16[2048,2048]{1,0:T(8,128)(2,1)} %wu_hbm.1, bf16[2048,2048]{1,0:T(8,128)(2,1)} %wd_hbm.1, f32[16,16]{1,0:T(8,128)} %gs.1, f32[16,16]{1,0:T(8,128)} %us.1, f32[16,16]{1,0:T(8,128)} %ds.1), custom_call_target="tpu_custom_call" | custom-call | tf_op jit(solution)/shard_map/pallas_call | solution.py:243
  42.7 1.5 %copy.9 = bf16[16,2048]{1,0:T(8,128)(2,1)} copy(bf16[16,2048]{1,0:T(8,128)(2,1)} %shard_map.73) | data formatting | bytes 131072
